TPU v7x, 256 devices: a whole 4x4x8 slice. The times are simulated.
256 devices in a mesh: prow: 32 (over x, y, core), pcol: 8 (over z).
Axes of the slice: x: 4, y: 4, z: 8, core: 2. Of those that a mesh axis runs over, the one named last changes fastest.
Arguments:
- right_side: float32 [4, 64, 256, 128], P(None, 'prow', 'pcol'), may hold values from -6 to 6
- diag_inverse: float32 [4, 64, 256, 256], P(None, 'prow', None, 'pcol'), as said below
- panels: float32 [3, 64, 8, 256, 256], P(None, 'prow', None, 'pcol'), may hold values from -0.125 to 0.125
- targets: int32 [3, 64, 8], P(None, 'prow'), may hold values from 64 to 255, as said below
Outputs:
- solution: float32 [4, 64, 256, 128], P(None, 'prow', 'pcol')
Inputs may be any that keep to these rules, and one draw needn't show every extreme that they name: targets[l, n, k] names a supernode of a level after l: it lies in (l + 1) * 64 to 255; repeats are allowed. diag_inverse is lower triangular with a diagonal in 0.5 to 1.5.
All inputs are finite; a program needn't handle non-finite values.
Results may differ from a plain program's by a relative error of at most 0.0001.
Values sent between devices are 32-bit elements; how exact they have to be, the bound alone decides.
A program may use at most 64 MiB of HBM per device.

v0:
```python
import jax
import jax.numpy as jnp
from jax import lax
from jax.sharding import PartitionSpec as P


def shards(right_side, diag_inverse, panels, targets):
    levels = right_side.shape[0]
    local_count = right_side.shape[1]
    own_rows = right_side.shape[2]
    columns = right_side.shape[3]
    blocks_off = panels.shape[2]
    level_count = local_count * lax.axis_size("prow")
    row_start = lax.axis_index("pcol") * own_rows
    updates = jnp.zeros((levels * level_count, own_rows, columns), jnp.float32)
    solved = []
    for level in range(levels):
        if level > 0:
            part_level = updates[level * level_count : (level + 1) * level_count]
            gathered = lax.psum_scatter(part_level, "prow", scatter_dimension=0, tiled=True)
            residual = right_side[level] - gathered
        else:
            residual = right_side[level]
        partial_sum = jnp.einsum(
            "nij,njr->nir", diag_inverse[level], residual, precision=lax.Precision.HIGHEST
        )
        last = level == levels - 1
        answer = lax.psum(partial_sum, "pcol")
        solved.append(lax.dynamic_slice_in_dim(answer, row_start, own_rows, 1))
        if not last:
            blocks = jnp.einsum(
                "nktj,njr->nktr", panels[level], answer, precision=lax.Precision.HIGHEST
            )
        if not last:
            places = targets[level].reshape(-1)
            updates = updates.at[places].add(
                blocks.reshape(local_count * blocks_off, own_rows, columns)
            )
    return jnp.stack(solved)


def solution(mesh):
    in_specs = (
        P(None, "prow", "pcol", None),
        P(None, "prow", None, "pcol"),
        P(None, "prow", None, "pcol", None),
        P(None, "prow", None),
    )
    out_specs = P(None, "prow", "pcol", None)
    return jax.shard_map(shards, mesh=mesh, in_specs=in_specs, out_specs=out_specs, check_vma=False)
```

profile of v0, /device:TPU:1, one launch (start us, length us, event | category | flops | bytes accessed | tf_op | source)
XLA Modules:
  0.0 585.5 jit_solution(8615570364964115895)
XLA Ops:
  6.5 2.1 fusion.15
  8.7 0.0 all-reduce.5.cloned.1.call-update
  8.7 0.0 reduce-scatter.4.cloned.1.call-start
  8.7 0.7 fusion.29
  9.5 0.1 reshape_squeeze.9
  9.5 72.0 %all-reduce.5.cloned.1.call-done = f32[2,256,128]{2,1,0:T(8,128)} async-done(((f32[2,256,128]{2,1,0:T(8,128)}), f32[2,256,128]{2,1,0:T(8,128)}) %all-reduce.5.cloned.1.call-update) | async-done | bytes 262160 | tf_op jit(solution)/shard_map/psum | solution.py:28
  81.5 1.7 fusion.4
  83.2 0.0 copy-start.3
  83.3 0.0 copy-start.4
  83.3 0.0 copy-start
  83.3 2.5 broadcast_in_dim.2
  85.7 2.4 scatter_fusion
  88.2 2.3 slice.68
  90.4 0.0 reduce-scatter.4.cloned.1.call-update
  90.5 0.0 all-reduce.7.cloned.1.call-start
  90.5 86.5 %reduce-scatter.4.cloned.1.call-done = f32[2,32,128]{2,1,0:T(8,128)} async-done(((f32[64,32,128]{2,1,0:T(8,128)}), f32[2,32,128]{2,1,0:T(8,128)}) %reduce-scatter.4.cloned.1.call-update) | async-done | bytes 32784 | tf_op jit(solution)/shard_map/reduce_scatter | solution.py:20
  177.0 1.9 convolution_bitcast_fusion.2
  178.9 0.0 all-reduce.7.cloned.1.call-update
  178.9 0.0 reduce-scatter.6.cloned.1.call-start
  179.0 0.1 reshape_squeeze.10
  179.1 69.3 %all-reduce.7.cloned.1.call-done = f32[2,256,128]{1,2,0:T(8,128)} async-done(((f32[2,256,128]{1,2,0:T(8,128)}), f32[2,256,128]{1,2,0:T(8,128)}) %all-reduce.7.cloned.1.call-update) | async-done | bytes 262160 | tf_op jit(solution)/shard_map/psum | solution.py:28
  248.4 1.6 fusion.2
  250.0 2.4 scatter_fusion.1
  252.4 2.3 slice.69
  254.7 0.0 reduce-scatter.6.cloned.1.call-update
  254.7 0.0 all-reduce.9.cloned.1.call-start
  254.8 86.5 %reduce-scatter.6.cloned.1.call-done = f32[2,32,128]{2,1,0:T(8,128)} async-done(((f32[64,32,128]{2,1,0:T(8,128)}), f32[2,32,128]{2,1,0:T(8,128)}) %reduce-scatter.6.cloned.1.call-update) | async-done | bytes 32784 | tf_op jit(solution)/shard_map/reduce_scatter | solution.py:20
  341.3 1.9 convolution_bitcast_fusion.1
  343.2 0.0 all-reduce.9.cloned.1.call-update
  343.2 0.0 reduce-scatter.8.cloned.1.call-start
  343.2 0.1 reshape_squeeze.11
  343.3 69.1 %all-reduce.9.cloned.1.call-done = f32[2,256,128]{1,2,0:T(8,128)} async-done(((f32[2,256,128]{1,2,0:T(8,128)}), f32[2,256,128]{1,2,0:T(8,128)}) %all-reduce.9.cloned.1.call-update) | async-done | bytes 262160 | tf_op jit(solution)/shard_map/psum | solution.py:28
  412.5 1.6 fusion
  414.1 2.4 scatter_fusion.2
  416.5 2.3 slice.70
  418.8 0.0 reduce-scatter.8.cloned.1.call-update
  418.8 0.0 all-reduce.11.cloned.1.call-start
  418.9 86.6 %reduce-scatter.8.cloned.1.call-done = f32[2,32,128]{2,1,0:T(8,128)} async-done(((f32[64,32,128]{2,1,0:T(8,128)}), f32[2,32,128]{2,1,0:T(8,128)}) %reduce-scatter.8.cloned.1.call-update) | async-done | bytes 32784 | tf_op jit(solution)/shard_map/reduce_scatter | solution.py:20
  505.4 1.9 convolution_bitcast_fusion
  507.3 0.0 all-reduce.11.cloned.1.call-update
  507.4 0.8 dynamic-slice_bitcast_fusion
  508.1 0.1 constant_dynamic-slice_fusion.2
  508.2 0.1 copy.7
  508.3 68.5 %all-reduce.11.cloned.1.call-done = f32[2,256,128]{1,2,0:T(8,128)} async-done(((f32[2,256,128]{1,2,0:T(8,128)}), f32[2,256,128]{1,2,0:T(8,128)}) %all-reduce.11.cloned.1.call-update) | async-done | bytes 262160 | tf_op jit(solution)/shard_map/psum | solution.py:28
  576.8 1.0 constant_dynamic-slice_fusion
  577.8 0.1 copy.11
  577.9 0.1 copy.9
  578.0 0.7 pad_maximum_fusion
  (11 shorter events, 0.0 us)
Async XLA Ops:
  6.5 75.0 %all-reduce.5.cloned.1.call-start = ((), (), s32[]{:S(2)}) async-start(), calls=%async_computation.3 | async-start | bytes 524288 | tf_op jit(solution)/shard_map/psum | solution.py:28
  8.7 168.3 %reduce-scatter.4.cloned.1.call-start = ((), (), s32[]{:S(2)}) async-start(), calls=%async_computation.4 | async-start | bytes 1081344 | tf_op jit(solution)/shard_map/reduce_scatter | solution.py:20
  83.2 93.8 %copy-start.3 = (f32[4,2,256,32]{2,3,1,0:T(8,128)S(1)}, f32[4,2,256,32]{2,3,1,0:T(8,128)}, u32[]{:S(2)}) copy-start(f32[4,2,256,32]{2,3,1,0:T(8,128)} %param.5) | copy-start | bytes 786436
  83.3 93.8 %copy-start.4 = (f32[4,2,32,128]{3,2,1,0:T(8,128)S(1)}, f32[4,2,32,128]{3,2,1,0:T(8,128)}, u32[]{:S(2)}) copy-start(f32[4,2,32,128]{3,2,1,0:T(8,128)} %param.4) | copy-start | bytes 393220
  83.3 165.2 %copy-start = (f32[3,2,8,32,256]{4,3,2,1,0:T(8,128)S(1)}, f32[3,2,8,32,256]{4,3,2,1,0:T(8,128)}, u32[]{:S(2)}) copy-start(f32[3,2,8,32,256]{4,3,2,1,0:T(8,128)} %param.6) | copy-start | bytes 4718596
  90.5 158.0 %all-reduce.7.cloned.1.call-start = ((), (), s32[]{:S(2)}) async-start(), calls=%async_computation.5 | async-start | bytes 524288 | tf_op jit(solution)/shard_map/psum | solution.py:28
  178.9 162.4 %reduce-scatter.6.cloned.1.call-start = ((), (), s32[]{:S(2)}) async-start(), calls=%async_computation.6 | async-start | bytes 1081344 | tf_op jit(solution)/shard_map/reduce_scatter | solution.py:20
  254.7 253.4 %copy-start.2 = (f32[2,256,128]{1,2,0:T(8,128)S(1)}, f32[2,256,128]{1,2,0:T(8,128)}, u32[]{:S(2)}) copy-start(f32[2,256,128]{1,2,0:T(8,128)} %all-reduce.7.cloned.1.call-done) | copy-start | bytes 786436
  254.7 157.8 %all-reduce.9.cloned.1.call-start = ((), (), s32[]{:S(2)}) async-start(), calls=%async_computation.7 | async-start | bytes 524288 | tf_op jit(solution)/shard_map/psum | solution.py:28
  343.2 162.2 %reduce-scatter.8.cloned.1.call-start = ((), (), s32[]{:S(2)}) async-start(), calls=%async_computation.8 | async-start | bytes 1081344 | tf_op jit(solution)/shard_map/reduce_scatter | solution.py:20
  412.5 164.3 %copy-start.1 = (f32[2,256,128]{1,2,0:T(8,128)S(1)}, f32[2,256,128]{1,2,0:T(8,128)}, u32[]{:S(2)}) copy-start(f32[2,256,128]{1,2,0:T(8,128)} %all-reduce.9.cloned.1.call-done) | copy-start | bytes 786436
  418.8 158.0 %all-reduce.11.cloned.1.call-start = ((), (), s32[]{:S(2)}) async-start(), calls=%async_computation.9 | async-start | bytes 524288 | tf_op jit(solution)/shard_map/psum | solution.py:28
Sparse Core Ops, SparseCore 0:
  9.7 71.7 all-reduce.4
  90.6 86.4 reduce-scatter.3
  179.4 69.0 all-reduce.6
  254.8 86.4 reduce-scatter.5
  343.5 68.9 all-reduce.8
  419.0 86.4 reduce-scatter.7
  507.8 69.0 all-reduce.10
where the time goes:
time: 590 us; the launch traced here: 586 us
  waiting for transfers between devices  539 us (91%)
  between operations  13.6 us (2%)
  matrix products  12.6 us (2%)
  local copies, waits for them, and re-layouts  12.3 us (2%)
  other arithmetic  7.99 us (1%)
    psum x4, waiting for transfers between devices, shards(): answer = lax.psum(partial_sum, 'pcol')  279 us
    reduce_scatter x3, waiting for transfers between devices, shards(): lax.psum_scatter(part_level, 'prow', scatter_dimension=0, tiled=True)  260 us
  transfers between devices with their start and end apart: 7, of which 7 were waited for; matrix products, arithmetic and copies ran while one was open for 0% of the time, Pallas kernels for 0%

commit v1 on v0

v1 whole, which is shorter than its diff:
```python
import functools

import jax
import jax.numpy as jnp
from jax import lax
from jax.experimental import pallas as pl
from jax.experimental.pallas import tpu as pltpu
from jax.sharding import PartitionSpec as P

MESH = pl.DeviceIdType.MESH
LEVELS = 4
STREAMS = 2
CH = 32
LANES = 128
HALF = 64
KB = 8


def dot(a, b):
    return lax.dot_general(
        a, b, (((1,), (0,)), ((), ())),
        precision=lax.Precision.HIGHEST, preferred_element_type=jnp.float32,
    )


def dot_t(a, b):
    return lax.dot_general(
        a, b, (((0,), (0,)), ((), ())),
        precision=lax.Precision.HIGHEST, preferred_element_type=jnp.float32,
    )


def kernel(
    nx, ny, nz,
    rhs_hbm, dinv_hbm, pan_hbm, tgt_hbm, out,
    tgt, rhs_v, dinv_v, pan_v, tbl_v, tbl_s, rp, rs_src, rs_dst, ag, dg, dgt, dbuf, dense, pr, xy, tmp,
    loc, rs_ss, rs_rs, ag_ss, ag_rs, dg_ss, dg_rs, pr_ss, pr_rs, xy_ss, xy_rs,
):
    chips = nx * ny
    width = CH * nz
    count = 4 * chips
    prow = lax.axis_index("prow")
    z = lax.axis_index("pcol")
    core = lax.rem(prow, 2)
    chip = prow // 2
    x = chip // ny
    y = lax.rem(chip, ny)

    def zpeer(k):
        return prow, lax.rem(z + k, nz)

    def xypeer(dx, dy):
        peer = lax.rem(x + dx, nx) * ny + lax.rem(y + dy, ny)
        return peer, (peer * 2 + core, z)

    sibling = (chip * 2 + 1 - core, z)
    offsets = [(dx, dy) for dx in range(nx) for dy in range(ny) if dx or dy]
    offsets.sort(key=lambda o: -(min(o[0], nx - o[0]) + min(o[1], ny - o[1])))
    zorder = sorted(range(1, nz), key=lambda k: -min(k, nz - k))

    def remote(src, dst, ss, rs, dev):
        return pltpu.make_async_remote_copy(
            src_ref=src, dst_ref=dst, send_sem=ss, recv_sem=rs, device_id=dev, device_id_type=MESH
        )

    due, sent = {}, []

    def arrived(*name):
        due.pop(name)()

    def wait_bytes(ref, sem):
        pltpu.make_async_copy(ref, ref, sem).wait()

    c_rhs = pltpu.make_async_copy(rhs_hbm, rhs_v, loc.at[0])
    c_dinv = pltpu.make_async_copy(dinv_hbm, dinv_v, loc.at[1])
    c_tgt = pltpu.make_async_copy(tgt_hbm, tgt, loc.at[6])
    c_tgt.start()
    c_rhs.start()
    c_dinv.start()
    for lev in range(LEVELS - 1):
        c = pltpu.make_async_copy(pan_hbm.at[lev], pan_v.at[lev], loc.at[2 + lev])
        c.start()
        due["pan", lev] = c.wait

    barrier = pltpu.get_barrier_semaphore()
    for k in zorder:
        pl.semaphore_signal(barrier, inc=1, device_id=zpeer(k), device_id_type=MESH)
    for dx, dy in offsets:
        pl.semaphore_signal(barrier, inc=1, device_id=xypeer(dx, dy)[1], device_id_type=MESH)
    pl.semaphore_signal(barrier, inc=1, device_id=sibling, device_id_type=MESH)

    lane = lax.broadcasted_iota(jnp.int32, (1, LANES), 1)
    low = lane < HALF

    c_tgt.wait()
    ids = lax.broadcasted_iota(jnp.int32, (1, LEVELS * count), 1)
    for row in range(2 * (LEVELS - 1)):
        found = jnp.full((1, LEVELS * count), KB, jnp.int32)
        for k in reversed(range(KB)):
            found = jnp.where(ids == tgt[row // 2, row % 2, k], k, found)
        tbl_v[pl.ds(row, 1), :] = found
    c_tbl = pltpu.make_async_copy(tbl_v, tbl_s, loc.at[5])
    c_tbl.start()
    due["tbl",] = c_tbl.wait

    for lev in range(LEVELS - 1):
        for s in range(STREAMS):
            for n in range(2):
                dbuf[lev, s, n, KB] = jnp.zeros((CH, LANES), jnp.float32)
    for i in range(2):
        for s in range(STREAMS):
            for j in range(nz):
                @pl.when(j >= z)
                def _():
                    rs_dst[i, s, j] = jnp.zeros((CH, LANES), jnp.float32)

    c_rhs.wait()
    for lev in range(LEVELS):
        r0, r1 = rhs_v[lev, 0], rhs_v[lev, 1]
        rp[lev, 0] = jnp.where(low, r0, pltpu.roll(r1, HALF, 1))
        rp[lev, 1] = jnp.where(low, pltpu.roll(r0, HALF, 1), r1)
    c_dinv.wait()

    def rs_compute(i, lev, s, res):
        p0 = dot_t(dinv_v[lev, 0], res)
        p1 = dot_t(dinv_v[lev, 1], res)
        rs_src[i, s] = jnp.where(low, p0, p1)

    def rs_arrive(i, s):
        for j in range(nz - 1):
            @pl.when(j < z)
            def _():
                wait_bytes(rs_dst.at[i, s, j], rs_rs.at[i, s, j])

    def rs_left(i, s):
        for k in range(1, nz):
            @pl.when(lax.rem(z + k, nz) > z)
            def _():
                wait_bytes(rs_src.at[i, s, pl.ds(0, CH)], rs_ss.at[i, s, k])

    def rs_send(i, s):
        due["rs", i, s] = lambda: rs_arrive(i, s)
        sent.append(lambda: rs_left(i, s))
        for k in zorder:
            dst = lax.rem(z + k, nz)

            @pl.when(dst > z)
            def _():
                remote(
                    rs_src.at[i, s, pl.ds(dst * CH, CH)], rs_dst.at[i, s, z],
                    rs_ss.at[i, s, k], rs_rs.at[i, s, z], (prow, dst),
                ).start()

    def rs_finish(i, s):
        acc = rs_src[i, s, pl.ds(z * CH, CH)]
        arrived("rs", i, s)
        for j in range(nz - 1):
            acc = acc + rs_dst[i, s, j]
        return acc

    def ag_send(lev, s, val):
        mine = pl.ds(z * CH, CH)
        others = ag.at[lev, s, pl.ds(0, (nz - 1) * CH)]
        due["ag", lev, s] = lambda: wait_bytes(others, ag_rs.at[lev, s])
        sent.append(lambda: wait_bytes(others, ag_ss.at[lev, s]))
        ag[lev, s, mine] = val
        for k in zorder:
            remote(
                ag.at[lev, s, mine], ag.at[lev, s, mine], ag_ss.at[lev, s], ag_rs.at[lev, s], zpeer(k)
            ).start()

    def ag_wait(lev, s):
        arrived("ag", lev, s)
        return ag[lev, s]

    half_steps = nz // 2

    def dg_copies(lev, step):
        d = lev - 1
        up, down = zpeer(1), zpeer(nz - 1)
        cu = lax.rem(z - step + nz, nz)
        cd = lax.rem(z + step, nz)
        res = []
        su = dg.at[d, :, pl.ds(cu * CH, CH)]
        sd = dg.at[d, :, pl.ds(cd * CH, CH)]
        if step < half_steps - 1:
            res.append(remote(su, su, dg_ss.at[d, step, 0], dg_rs.at[d, step, 0], up))
            res.append(remote(sd, sd, dg_ss.at[d, step, 1], dg_rs.at[d, step, 1], down))
        else:
            su = dg.at[d, 0, pl.ds(cu * CH, CH)]
            sd = dg.at[d, 1, pl.ds(cd * CH, CH)]
            res.append(remote(su, su, dg_ss.at[d, step, 0], dg_rs.at[d, step, 0], up))
            res.append(remote(sd, sd, dg_ss.at[d, step, 1], dg_rs.at[d, step, 1], down))
        return res

    def dg_step(lev, step):
        if step >= half_steps:
            return
        if step > 0:
            arrived("dg", lev, step - 1)
        else:
            dg[lev - 1, :, pl.ds(z * CH, CH)] = dinv_v[lev]
        copies = dg_copies(lev, step)
        due["dg", lev, step] = lambda: [c.wait_recv() for c in copies]
        sent.append(lambda: [c.wait_send() for c in copies])
        for c in copies:
            c.start()

    def dg_finish(lev):
        arrived("dg", lev, half_steps - 1)
        for n in range(2):
            dgt[n] = jnp.transpose(dg[lev - 1, n])

    def combine_panels(lev):
        arrived("pan", lev)
        for n in range(2):
            weight = {}
            for a in range(KB):
                for b in range(a + 1, KB):
                    same = tgt[lev, n, a] == tgt[lev, n, b]
                    weight[a, b] = jnp.where(same, 1.0, 0.0)

            def step(i, _, n=n, weight=weight):
                rows = pl.ds(pl.multiple_of(i * 8, 8), 8)
                vals = [pan_v[lev, n, k, rows] for k in range(KB)]
                for a in range(KB):
                    acc = vals[a]
                    for b in range(KB):
                        if b != a:
                            acc = acc + weight[min(a, b), max(a, b)] * vals[b]
                    pan_v[lev, n, a, rows] = acc
                return 0

            lax.fori_loop(0, CH // 8, step, 0)

    def gather(lev, level_to, s, side, b):
        q = core if side == 1 else 1 - core
        t = level_to * count + b * 4 + q * 2
        e0 = dbuf[lev, s, 0, tbl_s[2 * lev, t]] + dbuf[lev, s, 1, tbl_s[2 * lev + 1, t]]
        e1 = dbuf[lev, s, 0, tbl_s[2 * lev, t + 1]] + dbuf[lev, s, 1, tbl_s[2 * lev + 1, t + 1]]
        return jnp.where(low, e0, e1)

    def spread(lev, level_to, s, side):
        def step(b, _):
            val = gather(lev, level_to, s, side, b)
            if lev > 0:
                val = val + dense[level_to - 1, s, side, b]
            dense[level_to - 1, s, side, b] = val
            return 0

        lax.fori_loop(0, chips, step, 0, unroll=4)

    def solve(lev, s):
        r = ag_wait(lev, s)
        if lev > 0:
            a = jnp.where(low, dot(dgt[0], r), dot(dgt[1], r))
        else:
            a = r
        ar = pltpu.roll(a, HALF, 1)
        a0 = jnp.where(low, a, ar)
        a1 = jnp.where(low, ar, a)
        for n, an in ((0, a0), (1, a1)):
            d = dot(pan_v[lev, n].reshape(KB * CH, width), an)
            dbuf[lev, s, n, pl.ds(0, KB)] = d.reshape(KB, CH, LANES)
        spread(lev, lev + 1, s, 0)
        due["pr", lev, s] = lambda: wait_bytes(pr.at[lev, s], pr_rs.at[lev, s])
        sent.append(lambda: wait_bytes(pr.at[lev, s], pr_ss.at[lev, s]))
        remote(dense.at[lev, s, 0], pr.at[lev, s], pr_ss.at[lev, s], pr_rs.at[lev, s], sibling).start()
        tmp[0] = a0
        tmp[1] = a1
        cols = pl.ds(s * HALF, HALF)
        for n in range(2):
            out[lev, n, :, cols] = tmp[n, pl.ds(z * CH, CH), cols]
        spread(lev, lev + 1, s, 1)

    def send_xy(lev, s):
        arrived("pr", lev, s)

        def step(b, _):
            dense[lev, s, 1, b] = dense[lev, s, 1, b] + pr[lev, s, b]
            return 0

        lax.fori_loop(0, chips, step, 0, unroll=4)
        due["xy", lev, s] = lambda: wait_bytes(xy.at[lev, s], xy_rs.at[lev, s])
        sent.append(lambda: wait_bytes(xy.at[lev, s], xy_ss.at[lev, s]))
        for i, (dx, dy) in enumerate(offsets):
            peer, dev = xypeer(dx, dy)
            remote(dense.at[lev, s, 1, peer], xy.at[lev, s, i], xy_ss.at[lev, s], xy_rs.at[lev, s], dev).start()

    def residual(lev, s):
        arrived("xy", lev, s)
        acc = dense[lev, s, 1, chip]
        for i in range(len(offsets)):
            acc = acc + xy[lev, s, i]
        return rp[lev + 1, s] - acc

    for s in range(STREAMS):
        rs_compute(0, 0, s, rp[0, s])

    pl.semaphore_wait(barrier, nz - 1 + len(offsets) + 1)

    both = range(STREAMS)
    for s in both:
        rs_send(0, s)
    dg_step(1, 0)
    combine_panels(0)
    arrived("tbl")
    for s in both:
        ag_send(0, s, rs_finish(0, s))
    dg_step(1, 1)
    for lev in range(LEVELS - 1):
        for s in both:
            solve(lev, s)
        if lev == 0:
            dg_step(1, 2)
        elif lev == 1:
            dg_step(2, 2)
        for s in both:
            send_xy(lev, s)
        if lev == 0:
            dg_step(1, 3)
            dg_step(2, 0)
        elif lev == 1:
            dg_step(2, 3)
        for s in both:
            for to in range(lev + 2, LEVELS):
                for side in range(2):
                    spread(lev, to, s, side)
        if lev + 1 < LEVELS - 1:
            combine_panels(lev + 1)
            dg_finish(lev + 1)
            for s in both:
                ag_send(lev + 1, s, residual(lev, s))
            if lev == 0:
                dg_step(2, 1)
        else:
            for s in both:
                rs_compute(1, LEVELS - 1, s, residual(lev, s))
                rs_send(1, s)
    for s in both:
        a = rs_finish(1, s)
        ar = pltpu.roll(a, HALF, 1)
        cols = pl.ds(s * HALF, HALF)
        tmp[0, pl.ds(0, CH)] = jnp.where(low, a, ar)
        tmp[1, pl.ds(0, CH)] = jnp.where(low, ar, a)
        for n in range(2):
            out[LEVELS - 1, n, :, cols] = tmp[n, pl.ds(0, CH), cols]

    for wait in sent:
        wait()


def shards(nx, ny, nz, right_side, diag_inverse, panels, targets):
    chips = nx * ny
    width = CH * nz
    count = 4 * chips
    f32 = jnp.float32
    dma = pltpu.SemaphoreType.DMA
    hops = nz // 2
    hbm = pl.BlockSpec(memory_space=pltpu.HBM)
    return pl.pallas_call(
        functools.partial(kernel, nx, ny, nz),
        out_shape=jax.ShapeDtypeStruct((LEVELS, 2, CH, LANES), f32),
        in_specs=[hbm] * 4,
        out_specs=pl.BlockSpec(memory_space=pltpu.VMEM),
        scratch_shapes=[
            pltpu.SMEM((LEVELS - 1, 2, KB), jnp.int32),
            pltpu.VMEM((LEVELS, 2, CH, LANES), f32),
            pltpu.VMEM((LEVELS, 2, CH, width), f32),
            pltpu.VMEM((LEVELS - 1, 2, KB, CH, width), f32),
            pltpu.VMEM((8, LEVELS * count), jnp.int32),
            pltpu.SMEM((8, LEVELS * count), jnp.int32),
            pltpu.VMEM((LEVELS, STREAMS, CH, LANES), f32),
            pltpu.VMEM((2, STREAMS, width, LANES), f32),
            pltpu.VMEM((2, STREAMS, nz, CH, LANES), f32),
            pltpu.VMEM((LEVELS - 1, STREAMS, width, LANES), f32),
            pltpu.VMEM((2, 2, width, width), f32),
            pltpu.VMEM((2, width, width), f32),
            pltpu.VMEM((LEVELS - 1, STREAMS, 2, KB + 1, CH, LANES), f32),
            pltpu.VMEM((LEVELS - 1, STREAMS, 2, chips, CH, LANES), f32),
            pltpu.VMEM((LEVELS - 1, STREAMS, chips, CH, LANES), f32),
            pltpu.VMEM((LEVELS - 1, STREAMS, chips - 1, CH, LANES), f32),
            pltpu.VMEM((2, width, LANES), f32),
            dma((7,)),
            dma((2, STREAMS, nz)),
            dma((2, STREAMS, nz)),
            dma((LEVELS - 1, STREAMS)),
            dma((LEVELS - 1, STREAMS)),
            dma((2, hops, 2)),
            dma((2, hops, 2)),
            dma((LEVELS - 1, STREAMS)),
            dma((LEVELS - 1, STREAMS)),
            dma((LEVELS - 1, STREAMS)),
            dma((LEVELS - 1, STREAMS)),
        ],
        compiler_params=pltpu.CompilerParams(
            collective_id=0, has_side_effects=True, vmem_limit_bytes=60 * 1024 * 1024
        ),
    )(right_side, jnp.swapaxes(diag_inverse, 2, 3), panels, targets)


def solution(mesh):
    prow, nz = mesh.shape["prow"], mesh.shape["pcol"]
    ny = 4 if prow == 32 else 1
    nx = prow // (2 * ny)
    in_specs = (
        P(None, "prow", "pcol", None),
        P(None, "prow", None, "pcol"),
        P(None, "prow", None, "pcol", None),
        P(None, "prow", None),
    )
    return jax.shard_map(
        functools.partial(shards, nx, ny, nz), mesh=mesh, in_specs=in_specs,
        out_specs=P(None, "prow", "pcol", None), check_vma=False,
    )
```

time: 590 us -> 75.2 us (0.13)
  waiting for transfers between devices: 539 us -> 0 us
  Pallas kernels: 0 us -> 73.5 us
  between operations: 13.6 us -> 0.01 us
  matrix products: 12.6 us -> 0 us
  local copies, waits for them, and re-layouts: 12.3 us -> 1.57 us
  other arithmetic: 7.99 us -> 0 us
    psum x4 -> x0, waiting for transfers between devices: 279 us -> none  [shards(): answer = lax.psum(partial_sum, 'pcol')]
    reduce_scatter x3 -> x0, waiting for transfers between devices: 260 us -> none  [shards(): lax.psum_scatter(part_level, 'prow', scatter_dimension=0, tiled=True)]
    pallas_call x0 -> x1, Pallas kernels: none -> 73.5 us  [shards(): pl.pallas_call(functools.partial(kernel, nx, ny, nz), out_shape=jax.Shape...]
    dot_general x7 -> x0, matrix products: 12.6 us -> none  [the longest x4 7.74 us: shards(): jnp.einsum('nij,njr->nir', diag_inverse[level], residual, precision=lax.P...]
    slice x4 -> x0, local copies, waits for them, and re-layouts: 7.52 us -> none  [the longest x3 6.8 us: shards(): part_level = updates[level * level_count:(level + 1) * level_count]]
    scatter-add x3 -> x0, other arithmetic: 7.3 us -> none  [shards(): updates.at[places]]
  transfers between devices with their start and end apart: 7 -> 0, of which waited for: 7 -> 0; matrix products, arithmetic and copies ran while one was open for 0% -> 0% of each run, Pallas kernels for 0% -> 0%
where the time goes in v1:
time: 75.2 us; the launch traced here: 75.1 us
  Pallas kernels  73.5 us (98%)
  local copies, waits for them, and re-layouts  1.57 us (2%)
    pallas_call x1, Pallas kernels, shards(): pl.pallas_call(functools.partial(kernel, nx, ny, nz), out_shape=jax.Shape...  73.5 us
    unnamed x1, local copies, waits for them, and re-layouts  1.57 us

profile of v1, /device:TPU:1, one launch (start us, length us, event | category | flops | bytes accessed | tf_op | source)
XLA Modules:
  0.0 75.1 jit_solution(5370023891620188362)
XLA Ops:
  0.0 73.5 %shard_map.46 = f32[4,2,32,128]{3,2,1,0:T(8,128)} custom-call(f32[4,2,32,128]{3,2,1,0:T(8,128)} %rhs_hbm.1, f32[4,2,32,256]{3,2,1,0:T(8,128)} %bitcast.1, f32[3,2,8,32,256]{4,3,2,1,0:T(8,128)} %pan_hbm.1, s32[3,2,8]{2,1,0:T(2,128)} %tgt_hbm.1), custom_call_target="tpu_custom_call" | custom-call | tf_op jit(solution)/shard_map/pallas_call | solution.py:361
  73.5 1.6 %copy.6 = f32[4,2,32,128]{3,2,1,0:T(8,128)} copy(f32[4,2,32,128]{3,2,1,0:T(8,128)} %shard_map.46) | data formatting | bytes 262144

commit v2 on v1

v2 whole, which is shorter than its diff:
```python
import functools

import jax
import jax.numpy as jnp
from jax import lax
from jax.experimental import pallas as pl
from jax.experimental.pallas import tpu as pltpu
from jax.sharding import PartitionSpec as P

MESH = pl.DeviceIdType.MESH
LEVELS = 4
CH = 32
LANES = 128
HALF = 64
KB = 8


def split(a):
    hi = a.astype(jnp.bfloat16)
    return hi, (a - hi.astype(jnp.float32)).astype(jnp.bfloat16)


def dot3(a, b, dims):
    ah, al = split(a)
    bh, bl = split(b)
    f = functools.partial(
        lax.dot_general, dimension_numbers=(dims, ((), ())), preferred_element_type=jnp.float32
    )
    return f(ah, bh) + (f(ah, bl) + f(al, bh))


def dot(a, b):
    return dot3(a, b, ((1,), (0,)))


def dot_t(a, b):
    return dot3(a, b, ((0,), (0,)))


def kernel(
    nx, ny, nz,
    rhs_hbm, dinv_hbm, pan_hbm, tgt_hbm, out,
    tgt, rhs_v, dinv_v, dinv_x, pan_v, tbl_v, tbl_s, rp, rq, rs_src, rs_dst, av, ag, dg, dgt,
    dbuf, dense, xy, tmp, yv, yx,
    loc, rs_ss, rs_rs, ag_ss, ag_rs, dg_ss, dg_rs, xy_ss, xy_rs, sib_ss, sib_rs,
):
    chips = nx * ny
    width = CH * nz
    count = 4 * chips
    prow = lax.axis_index("prow")
    z = lax.axis_index("pcol")
    core = lax.rem(prow, 2)
    chip = prow // 2
    x = chip // ny
    y = lax.rem(chip, ny)
    both = range(2)
    mine = pl.ds(z * CH, CH)

    def zpeer(k):
        return prow, lax.rem(z + k, nz)

    def xypeer(dx, dy):
        peer = lax.rem(x + dx, nx) * ny + lax.rem(y + dy, ny)
        return peer, (peer * 2 + core, z)

    sibling = (chip * 2 + 1 - core, z)
    offsets = [(dx, dy) for dx in range(nx) for dy in range(ny) if dx or dy]
    offsets.sort(key=lambda o: -(min(o[0], nx - o[0]) + min(o[1], ny - o[1])))
    zorder = sorted(range(1, nz), key=lambda k: -min(k, nz - k))

    def remote(src, dst, ss, rs, dev):
        return pltpu.make_async_remote_copy(
            src_ref=src, dst_ref=dst, send_sem=ss, recv_sem=rs, device_id=dev, device_id_type=MESH
        )

    due, sent = {}, []

    def arrived(*name):
        due.pop(name)()

    def wait_bytes(ref, sem):
        pltpu.make_async_copy(ref, ref, sem).wait()

    c_rhs = pltpu.make_async_copy(rhs_hbm, rhs_v, loc.at[0])
    c_dinv = pltpu.make_async_copy(dinv_hbm, dinv_v, loc.at[1])
    c_tgt = pltpu.make_async_copy(tgt_hbm, tgt, loc.at[6])
    c_tgt.start()
    c_rhs.start()
    c_dinv.start()
    for lev in range(LEVELS - 1):
        c = pltpu.make_async_copy(pan_hbm.at[lev], pan_v.at[lev, core], loc.at[2 + lev])
        c.start()
        due["pan", lev] = c.wait

    barrier = pltpu.get_barrier_semaphore()
    for k in zorder:
        for c in both:
            pl.semaphore_signal(
                barrier, inc=1, device_id=(chip * 2 + c, lax.rem(z + k, nz)), device_id_type=MESH
            )
    for dx, dy in offsets:
        pl.semaphore_signal(barrier, inc=1, device_id=xypeer(dx, dy)[1], device_id_type=MESH)
    pl.semaphore_signal(barrier, inc=1, device_id=sibling, device_id_type=MESH)

    lane = lax.broadcasted_iota(jnp.int32, (1, LANES), 1)
    low = lane < HALF

    def sib_send(i, src, dst):
        c = remote(src, dst, sib_ss.at[i], sib_rs.at[i], sibling)
        c.start()
        due["sib", i] = c.wait_recv
        sent.append(c.wait_send)

    c_rhs.wait()
    for lev in range(LEVELS):
        r0, r1 = rhs_v[lev, 0], rhs_v[lev, 1]
        rp[0, lev] = jnp.where(low, r0, pltpu.roll(r1, HALF, 1))
        rp[1, lev] = jnp.where(low, pltpu.roll(r0, HALF, 1), r1)
    c_dinv.wait()
    for s in both:
        r = rp[s, 0]
        rs_src[0, s] = jnp.where(low, dot_t(dinv_v[0, 0], r), dot_t(dinv_v[0, 1], r))

    c_tgt.wait()
    ids = lax.broadcasted_iota(jnp.int32, (1, LEVELS * count), 1)
    for row in range(8):
        found = jnp.full((1, LEVELS * count), KB, jnp.int32)
        if row < 2 * (LEVELS - 1):
            for k in reversed(range(KB)):
                found = jnp.where(ids == tgt[row // 2, row % 2, k], k, found)
        tbl_v[core, pl.ds(row, 1), :] = found

    for lev in range(LEVELS - 1):
        for m in range(4):
            dbuf[lev, m, KB] = jnp.zeros((CH, LANES), jnp.float32)
    for s in both:
        for j in range(nz):
            @pl.when(j >= z)
            def _():
                rs_dst[0, s, j] = jnp.zeros((CH, LANES), jnp.float32)

            @pl.when((j > z) | ((j == z) & (core == s)))
            def _():
                rs_dst[1, s, j] = jnp.zeros((CH, LANES), jnp.float32)

    def rs_send(i, s):
        owner = prow if i == 0 else chip * 2 + s
        slot = s if i == 0 else core

        def arrive():
            for j in range(nz):
                came = j < z
                if i == 1:
                    came = came | ((j == z) & (core != s))

                @pl.when(came)
                def _():
                    wait_bytes(rs_dst.at[i, s, j], rs_rs.at[i, s, j])

        def left():
            for k in range(nz):
                went = lax.rem(z + k, nz) > z if k else core != s
                if k or i == 1:
                    @pl.when(went)
                    def _():
                        wait_bytes(rs_src.at[i, s, pl.ds(0, CH)], rs_ss.at[i, s, k])

        due["rs", i, s] = arrive
        sent.append(left)
        for k in zorder:
            dst = lax.rem(z + k, nz)

            @pl.when(dst > z)
            def _():
                remote(
                    rs_src.at[i, s, pl.ds(dst * CH, CH)], rs_dst.at[i, slot, z],
                    rs_ss.at[i, s, k], rs_rs.at[i, slot, z], (owner, dst),
                ).start()
        if i == 1:
            @pl.when(core != s)
            def _():
                remote(
                    rs_src.at[i, s, mine], rs_dst.at[i, slot, z],
                    rs_ss.at[i, s, 0], rs_rs.at[i, slot, z], sibling,
                ).start()

    def rs_finish(i, s):
        arrived("rs", i, s)
        acc = rs_src[i, s, mine]
        if i == 1:
            acc = jnp.where(core == s, acc, rs_dst[i, s, nz - 1])
        for j in range(nz - 1):
            acc = acc + rs_dst[i, s, j]
        return acc

    def write(lev, x0, x1):
        out[lev, 0] = jnp.where(low, x0, pltpu.roll(x1, HALF, 1))
        out[lev, 1] = jnp.where(low, pltpu.roll(x0, HALF, 1), x1)

    def chunks(lev, p, n):
        return ag.at[lev, p, pl.ds(0, n * CH)]

    def ag_first(s, val):
        def arrive():
            @pl.when(core == s)
            def _():
                wait_bytes(chunks(0, s, nz - 1), ag_rs.at[0, s])

            @pl.when(core != s)
            def _():
                wait_bytes(chunks(0, s, nz), ag_rs.at[0, s])

        def left():
            wait_bytes(chunks(0, s, nz - 1), ag_ss.at[0, s])

            @pl.when(core != s)
            def _():
                wait_bytes(av.at[s], sib_ss.at[AV])

        due["ag", 0, s] = arrive
        sent.append(left)
        av[s] = val
        dst = ag.at[0, core, mine]
        for k in zorder:
            remote(
                av.at[s], dst, ag_ss.at[0, s], ag_rs.at[0, core], (chip * 2 + s, lax.rem(z + k, nz))
            ).start()

        @pl.when(core != s)
        def _():
            remote(av.at[s], dst, sib_ss.at[AV], ag_rs.at[0, core], sibling).start()

        @pl.when(core == s)
        def _():
            ag[0, core, mine] = val

    def ag_send(lev, p, val):
        others = chunks(lev, p, nz - 1)
        due["ag", lev, p] = lambda: wait_bytes(others, ag_rs.at[lev, p])
        sent.append(lambda: wait_bytes(others, ag_ss.at[lev, p]))
        ag[lev, p, mine] = val
        part = ag.at[lev, p, mine]
        for k in zorder:
            remote(part, part, ag_ss.at[lev, p], ag_rs.at[lev, p], zpeer(k)).start()

    half_steps = nz // 2

    def dg_copies(lev, step):
        d = lev - 1
        cu = lax.rem(z - step + nz, nz)
        cd = lax.rem(z + step, nz)
        if step < half_steps - 1:
            su = dg.at[d, :, pl.ds(cu * CH, CH)]
            sd = dg.at[d, :, pl.ds(cd * CH, CH)]
        else:
            su = dg.at[d, 0, pl.ds(cu * CH, CH)]
            sd = dg.at[d, 1, pl.ds(cd * CH, CH)]
        return [
            remote(su, su, dg_ss.at[d, step, 0], dg_rs.at[d, step, 0], zpeer(1)),
            remote(sd, sd, dg_ss.at[d, step, 1], dg_rs.at[d, step, 1], zpeer(nz - 1)),
        ]

    def dg_step(lev, step):
        if step >= half_steps or lev > 2:
            return
        if step > 0:
            arrived("dg", lev, step - 1)
        else:
            dg[lev - 1, :, mine] = dinv_v[lev]
        copies = dg_copies(lev, step)
        due["dg", lev, step] = lambda: [c.wait_recv() for c in copies]
        sent.append(lambda: [c.wait_send() for c in copies])
        for c in copies:
            c.start()

    def dg_finish(lev):
        arrived("dg", lev, half_steps - 1)
        for n in both:
            dgt[lev - 1, core, n] = jnp.transpose(dg[lev - 1, n])
        sib_send(DGT + lev, dgt.at[lev - 1, core], dgt.at[lev - 1, core])

    def combine_panels(lev):
        arrived("pan", lev)
        for n in both:
            weight = {}
            for a in range(KB):
                for b in range(a + 1, KB):
                    same = tgt[lev, n, a] == tgt[lev, n, b]
                    weight[a, b] = jnp.where(same, 1.0, 0.0)

            def step(i, _, n=n, weight=weight):
                rows = pl.ds(pl.multiple_of(i * 8, 8), 8)
                vals = [pan_v[lev, core, n, k, rows] for k in range(KB)]
                for a in range(KB):
                    acc = vals[a]
                    for b in range(KB):
                        if b != a:
                            acc = acc + weight[min(a, b), max(a, b)] * vals[b]
                    pan_v[lev, core, n, a, rows] = acc
                return 0

            lax.fori_loop(0, CH // 8, step, 0)
        sib_send(PAN + lev, pan_v.at[lev, core], pan_v.at[lev, core])

    def gather(lev, level_to, p, b):
        t = level_to * count + b * 4 + p * 2
        e = [None, None]
        for j in both:
            for m in range(4):
                block = dbuf[lev, m, tbl_s[m // 2, 2 * lev + m % 2, t + j]]
                e[j] = block if m == 0 else e[j] + block
        return jnp.where(low, e[0], e[1])

    def spread(lev, level_to, p):
        group = min(chips, 4)

        def step(i, _):
            vals = []
            for j in range(group):
                b = i * group + j
                val = gather(lev, level_to, p, b)
                if lev > 0:
                    val = val + dense[level_to - 1, p, b]
                vals.append(val)
            for j, val in enumerate(vals):
                dense[level_to - 1, p, i * group + j] = val
            return 0

        lax.fori_loop(0, chips // group, step, 0, unroll=True)

    def solve(lev, p):
        arrived("ag", lev, p)
        a = ag[lev, p]
        if lev > 0:
            a = jnp.where(low, dot(dgt[lev - 1, p, 0], a), dot(dgt[lev - 1, p, 1], a))
            tmp[...] = a
            yv[lev - 1, p] = tmp[mine]
        ar = pltpu.roll(a, HALF, 1)
        for n, an in ((0, jnp.where(low, a, ar)), (1, jnp.where(low, ar, a))):
            d = dot(pan_v[lev, p, n].reshape(KB * CH, width), an)
            dbuf[lev, 2 * p + n, pl.ds(0, KB)] = d.reshape(KB, CH, LANES)

    def xy_send(lev, p):
        due["xy", lev, p] = lambda: wait_bytes(xy.at[lev, p], xy_rs.at[lev, p])
        sent.append(lambda: wait_bytes(xy.at[lev, p], xy_ss.at[lev, p]))
        for i, (dx, dy) in enumerate(offsets):
            peer, dev = xypeer(dx, dy)
            remote(dense.at[lev, p, peer], xy.at[lev, p, i], xy_ss.at[lev, p], xy_rs.at[lev, p], dev).start()

    def residual(lev, p):
        arrived("xy", lev, p)
        acc = dense[lev, p, chip]
        for i in range(len(offsets)):
            acc = acc + xy[lev, p, i]
        return rq[p, lev] - acc

    pl.semaphore_wait(barrier, 2 * (nz - 1) + len(offsets) + 1)

    for s in both:
        rs_send(0, s)
    sib_send(TBL, tbl_v.at[core], tbl_v.at[core])
    sib_send(RHS, rp.at[1 - core, pl.ds(1, LEVELS - 1)], rq.at[core])
    sib_send(INV, dinv_v.at[LEVELS - 1], dinv_x.at[core])
    rq[core] = rp[core, pl.ds(1, LEVELS - 1)]
    dinv_x[core] = dinv_v[LEVELS - 1]
    dg_step(1, 0)
    combine_panels(0)
    first = []
    for s in both:
        val = rs_finish(0, s)
        ag_first(s, val)
        first.append(val)
    dg_step(1, 1)
    write(0, *first)
    arrived("sib", TBL)
    c_tbl = pltpu.make_async_copy(tbl_v, tbl_s, loc.at[5])
    c_tbl.start()
    combine_panels(1)
    combine_panels(2)
    c_tbl.wait()
    arrived("sib", RHS)
    arrived("sib", INV)
    for lev in range(LEVELS - 1):
        arrived("sib", PAN + lev)
        if lev > 0:
            arrived("sib", DGT + lev)
        solve(lev, 0)
        dg_step(lev + 1, 2)
        solve(lev, 1)
        for p in both:
            spread(lev, lev + 1, p)
            xy_send(lev, p)
        dg_step(lev + 1, 3)
        dg_step(lev + 2, 0)
        if lev > 0:
            sib_send(ANS + lev, yv.at[lev - 1, 1 - core], yx.at[lev - 1])
        for to in range(lev + 2, LEVELS):
            for p in both:
                spread(lev, to, p)
        if lev < LEVELS - 2:
            dg_finish(lev + 1)
            for p in both:
                ag_send(lev + 1, p, residual(lev, p))
            dg_step(lev + 2, 1)
        else:
            for p in both:
                r = residual(lev, p)
                rs_src[1, p] = jnp.where(low, dot_t(dinv_x[p, 0], r), dot_t(dinv_x[p, 1], r))
                rs_send(1, p)
    for lev in (1, 2):
        arrived("sib", ANS + lev)
        own, other = yv[lev - 1, core], yx[lev - 1]
        write(lev, jnp.where(core == 0, own, other), jnp.where(core == 0, other, own))
    write(LEVELS - 1, rs_finish(1, 0), rs_finish(1, 1))

    for wait in sent:
        wait()


TBL, RHS, INV, AV, PAN, DGT, ANS, SIBS = 0, 1, 2, 3, 4, 6, 8, 11


def shards(nx, ny, nz, right_side, diag_inverse, panels, targets):
    chips = nx * ny
    width = CH * nz
    count = 4 * chips
    f32 = jnp.float32
    dma = pltpu.SemaphoreType.DMA
    vmem = pltpu.VMEM
    hops = nz // 2
    solved = LEVELS - 1
    hbm = pl.BlockSpec(memory_space=pltpu.HBM)
    return pl.pallas_call(
        functools.partial(kernel, nx, ny, nz),
        out_shape=jax.ShapeDtypeStruct((LEVELS, 2, CH, LANES), f32),
        in_specs=[hbm] * 4,
        out_specs=pl.BlockSpec(memory_space=pltpu.VMEM),
        scratch_shapes=[
            pltpu.SMEM((solved, 2, KB), jnp.int32),
            vmem((LEVELS, 2, CH, LANES), f32),
            vmem((LEVELS, 2, CH, width), f32),
            vmem((2, 2, CH, width), f32),
            vmem((solved, 2, 2, KB, CH, width), f32),
            vmem((2, 8, LEVELS * count), jnp.int32),
            pltpu.SMEM((2, 8, LEVELS * count), jnp.int32),
            vmem((2, LEVELS, CH, LANES), f32),
            vmem((2, solved, CH, LANES), f32),
            vmem((2, 2, width, LANES), f32),
            vmem((2, 2, nz, CH, LANES), f32),
            vmem((2, CH, LANES), f32),
            vmem((solved, 2, width, LANES), f32),
            vmem((2, 2, width, width), f32),
            vmem((2, 2, 2, width, width), f32),
            vmem((solved, 4, KB + 1, CH, LANES), f32),
            vmem((solved, 2, chips, CH, LANES), f32),
            vmem((solved, 2, chips - 1, CH, LANES), f32),
            vmem((width, LANES), f32),
            vmem((2, 2, CH, LANES), f32),
            vmem((2, CH, LANES), f32),
            dma((7,)),
            dma((2, 2, nz)),
            dma((2, 2, nz)),
            dma((solved, 2)),
            dma((solved, 2)),
            dma((2, hops, 2)),
            dma((2, hops, 2)),
            dma((solved, 2)),
            dma((solved, 2)),
            dma((SIBS,)),
            dma((SIBS,)),
        ],
        compiler_params=pltpu.CompilerParams(
            collective_id=0, has_side_effects=True, vmem_limit_bytes=60 * 1024 * 1024
        ),
    )(right_side, jnp.swapaxes(diag_inverse, 2, 3), panels, targets)


def solution(mesh):
    prow, nz = mesh.shape["prow"], mesh.shape["pcol"]
    ny = 4 if prow == 32 else 1
    nx = prow // (2 * ny)
    in_specs = (
        P(None, "prow", "pcol", None),
        P(None, "prow", None, "pcol"),
        P(None, "prow", None, "pcol", None),
        P(None, "prow", None),
    )
    return jax.shard_map(
        functools.partial(shards, nx, ny, nz), mesh=mesh, in_specs=in_specs,
        out_specs=P(None, "prow", "pcol", None), check_vma=False,
    )
```

time: 75.2 us -> 70.3 us (0.935)
  Pallas kernels: 73.5 us -> 68.5 us
    pallas_call x1, Pallas kernels: 73.5 us -> 68.5 us  [shards(): pl.pallas_call(functools.partial(kernel, nx, ny, nz), out_shape=jax.Shape...]
where the time goes in v2:
time: 70.3 us; the launch traced here: 70.1 us
  Pallas kernels  68.5 us (97%)
  local copies, waits for them, and re-layouts  1.57 us (2%)
    pallas_call x1, Pallas kernels, shards(): pl.pallas_call(functools.partial(kernel, nx, ny, nz), out_shape=jax.Shape...  68.5 us
    unnamed x1, local copies, waits for them, and re-layouts  1.57 us

profile of v2, /device:TPU:1, one launch (start us, length us, event | category | flops | bytes accessed | tf_op | source)
XLA Modules:
  0.0 70.1 jit_solution(1353530325370786345)
XLA Ops:
  0.0 68.5 %shard_map.46 = f32[4,2,32,128]{3,2,1,0:T(8,128)} custom-call(f32[4,2,32,128]{3,2,1,0:T(8,128)} %rhs_hbm.1, f32[4,2,32,256]{3,2,1,0:T(8,128)} %bitcast.1, f32[3,2,8,32,256]{4,3,2,1,0:T(8,128)} %pan_hbm.1, s32[3,2,8]{2,1,0:T(2,128)} %tgt_hbm.1), custom_call_target="tpu_custom_call" | custom-call | tf_op jit(solution)/shard_map/pallas_call | solution.py:433
  68.5 1.6 %copy.6 = f32[4,2,32,128]{3,2,1,0:T(8,128)} copy(f32[4,2,32,128]{3,2,1,0:T(8,128)} %shard_map.46) | data formatting | bytes 262144

commit v3 on v2

--- a/solution.py
+++ b/solution.py
@@ -26,7 +26,9 @@
     f = functools.partial(
         lax.dot_general, dimension_numbers=(dims, ((), ())), preferred_element_type=jnp.float32
     )
-    return f(ah, bh) + (f(ah, bl) + f(al, bh))
+    n = b.shape[1]
+    wide = f(ah, jnp.concatenate([bh, bl], axis=1))
+    return wide[:, :n] + (wide[:, n:] + f(al, bh))
 
 
 def dot(a, b):
@@ -40,9 +42,9 @@
 def kernel(
     nx, ny, nz,
     rhs_hbm, dinv_hbm, pan_hbm, tgt_hbm, out,
-    tgt, rhs_v, dinv_v, dinv_x, pan_v, tbl_v, tbl_s, rp, rq, rs_src, rs_dst, av, ag, dg, dgt,
-    dbuf, dense, xy, tmp, yv, yx,
-    loc, rs_ss, rs_rs, ag_ss, ag_rs, dg_ss, dg_rs, xy_ss, xy_rs, sib_ss, sib_rs,
+    tgt, rhs_v, dinv_v, dinv_x, pan_v, tbl_v, tbl_s, rp, rqp, rq, rs_src, rs_dst, fs_src, fs_dst, av, ag, dg, dgt,
+    dbuf, dense, xy, tmp, yv, yo, yx,
+    loc, rs_ss, rs_rs, fs_ss, fs_rs, ag_ss, ag_rs, dg_ss, dg_rs, xy_ss, xy_rs, sib_ss, sib_rs,
 ):
     chips = nx * ny
     width = CH * nz
@@ -104,6 +106,25 @@
 
     lane = lax.broadcasted_iota(jnp.int32, (1, LANES), 1)
     low = lane < HALF
+    first_q, third_q = lane < HALF // 2, lane < HALF // 2 * 3
+
+    def quarters(a, b, c, d):
+        return jnp.where(low, jnp.where(first_q, a, b), jnp.where(third_q, c, d))
+
+    def turn(v, k):
+        return pltpu.roll(v, k % 4 * (HALF // 2), 1) if k % 4 else v
+
+    def to_streams(v, w):
+        return (
+            quarters(v, turn(v, -1), turn(w, 2), turn(w, 1)),
+            quarters(turn(v, -1), turn(v, -2), turn(w, 1), w),
+        )
+
+    def to_packs(v, w):
+        return (
+            quarters(v, turn(w, 1), turn(v, 1), turn(w, 2)),
+            quarters(turn(v, -2), turn(w, -1), turn(v, -1), w),
+        )
 
     def sib_send(i, src, dst):
         c = remote(src, dst, sib_ss.at[i], sib_rs.at[i], sibling)
@@ -119,7 +140,7 @@
     c_dinv.wait()
     for s in both:
         r = rp[s, 0]
-        rs_src[0, s] = jnp.where(low, dot_t(dinv_v[0, 0], r), dot_t(dinv_v[0, 1], r))
+        rs_src[s] = jnp.where(low, dot_t(dinv_v[0, 0], r), dot_t(dinv_v[0, 1], r))
 
     c_tgt.wait()
     ids = lax.broadcasted_iota(jnp.int32, (1, LEVELS * count), 1)
@@ -131,41 +152,34 @@
         tbl_v[core, pl.ds(row, 1), :] = found
 
     for lev in range(LEVELS - 1):
-        for m in range(4):
-            dbuf[lev, m, KB] = jnp.zeros((CH, LANES), jnp.float32)
+        for u in both:
+            for m in range(4):
+                dbuf[lev, u, m, KB] = jnp.zeros((CH, LANES), jnp.float32)
     for s in both:
         for j in range(nz):
             @pl.when(j >= z)
             def _():
-                rs_dst[0, s, j] = jnp.zeros((CH, LANES), jnp.float32)
+                rs_dst[s, j] = jnp.zeros((CH, LANES), jnp.float32)
 
             @pl.when((j > z) | ((j == z) & (core == s)))
             def _():
-                rs_dst[1, s, j] = jnp.zeros((CH, LANES), jnp.float32)
-
-    def rs_send(i, s):
-        owner = prow if i == 0 else chip * 2 + s
-        slot = s if i == 0 else core
-
+                for u in both:
+                    fs_dst[u, s, j] = jnp.zeros((CH // 2, LANES), jnp.float32)
+
+    def rs_send(s):
         def arrive():
-            for j in range(nz):
-                came = j < z
-                if i == 1:
-                    came = came | ((j == z) & (core != s))
-
-                @pl.when(came)
+            for j in range(nz - 1):
+                @pl.when(j < z)
                 def _():
-                    wait_bytes(rs_dst.at[i, s, j], rs_rs.at[i, s, j])
+                    wait_bytes(rs_dst.at[s, j], rs_rs.at[s, j])
 
         def left():
-            for k in range(nz):
-                went = lax.rem(z + k, nz) > z if k else core != s
-                if k or i == 1:
-                    @pl.when(went)
-                    def _():
-                        wait_bytes(rs_src.at[i, s, pl.ds(0, CH)], rs_ss.at[i, s, k])
-
-        due["rs", i, s] = arrive
+            for k in range(1, nz):
+                @pl.when(lax.rem(z + k, nz) > z)
+                def _():
+                    wait_bytes(rs_src.at[s, pl.ds(0, CH)], rs_ss.at[s, k])
+
+        due["rs", s] = arrive
         sent.append(left)
         for k in zorder:
             dst = lax.rem(z + k, nz)
@@ -173,25 +187,59 @@
             @pl.when(dst > z)
             def _():
                 remote(
-                    rs_src.at[i, s, pl.ds(dst * CH, CH)], rs_dst.at[i, slot, z],
-                    rs_ss.at[i, s, k], rs_rs.at[i, slot, z], (owner, dst),
+                    rs_src.at[s, pl.ds(dst * CH, CH)], rs_dst.at[s, z],
+                    rs_ss.at[s, k], rs_rs.at[s, z], (prow, dst),
                 ).start()
-        if i == 1:
-            @pl.when(core != s)
-            def _():
-                remote(
-                    rs_src.at[i, s, mine], rs_dst.at[i, slot, z],
-                    rs_ss.at[i, s, 0], rs_rs.at[i, slot, z], sibling,
-                ).start()
-
-    def rs_finish(i, s):
-        arrived("rs", i, s)
-        acc = rs_src[i, s, mine]
-        if i == 1:
-            acc = jnp.where(core == s, acc, rs_dst[i, s, nz - 1])
+
+    def rs_finish(s):
+        arrived("rs", s)
+        acc = rs_src[s, mine]
         for j in range(nz - 1):
-            acc = acc + rs_dst[i, s, j]
+            acc = acc + rs_dst[s, j]
         return acc
+
+    def fs_send(u, r):
+        p = quarters(*[dot_t(dinv_x[m // 2, m % 2], r) for m in range(4)])
+        for b in range(nz):
+            top, bottom = p[b * CH : b * CH + CH // 2], p[b * CH + CH // 2 : (b + 1) * CH]
+            fs_src[u, 0, b] = jnp.where(low, top, turn(bottom, 2))
+            fs_src[u, 1, b] = jnp.where(low, turn(top, 2), bottom)
+
+        def arrive():
+            for h in both:
+                for j in range(nz):
+                    @pl.when((j < z) | ((j == z) & (core != h)))
+                    def _():
+                        wait_bytes(fs_dst.at[u, h, j], fs_rs.at[u, h, j])
+
+        def left():
+            for q in both:
+                for k in range(nz):
+                    @pl.when(lax.rem(z + k, nz) > z if k else core != q)
+                    def _():
+                        wait_bytes(fs_src.at[u, q, 0], fs_ss.at[u, q, k])
+
+        due["fs", u] = arrive
+        sent.append(left)
+        for k in zorder + [0]:
+            dst = lax.rem(z + k, nz)
+            for q in both:
+                @pl.when(dst > z if k else core != q)
+                def _():
+                    remote(
+                        fs_src.at[u, q, dst], fs_dst.at[u, core, z],
+                        fs_ss.at[u, q, k], fs_rs.at[u, core, z], (chip * 2 + q, dst),
+                    ).start()
+
+    def fs_finish(u):
+        arrived("fs", u)
+        res = []
+        for h in both:
+            acc = jnp.where(core == h, fs_src[u, h, z], fs_dst[u, h, nz - 1])
+            for j in range(nz - 1):
+                acc = acc + fs_dst[u, h, j]
+            res.append(jnp.concatenate([acc, turn(acc, 2)], axis=0))
+        return res
 
     def write(lev, x0, x1):
         out[lev, 0] = jnp.where(low, x0, pltpu.roll(x1, HALF, 1))
@@ -243,25 +291,26 @@
         for k in zorder:
             remote(part, part, ag_ss.at[lev, p], ag_rs.at[lev, p], zpeer(k)).start()
 
-    half_steps = nz // 2
+    relays = {
+        8: [
+            [(0, 1, None), (0, -1, None)],
+            [(-1, 1, None), (1, -1, None)],
+            [(-2, 2, 0), (2, -2, 1), (-2, 1, None), (2, -1, None)],
+        ],
+        4: [[(0, 1, None), (0, -1, None)], [(-1, 1, 0), (1, -1, 1)]],
+    }[nz]
 
     def dg_copies(lev, step):
         d = lev - 1
-        cu = lax.rem(z - step + nz, nz)
-        cd = lax.rem(z + step, nz)
-        if step < half_steps - 1:
-            su = dg.at[d, :, pl.ds(cu * CH, CH)]
-            sd = dg.at[d, :, pl.ds(cd * CH, CH)]
-        else:
-            su = dg.at[d, 0, pl.ds(cu * CH, CH)]
-            sd = dg.at[d, 1, pl.ds(cd * CH, CH)]
-        return [
-            remote(su, su, dg_ss.at[d, step, 0], dg_rs.at[d, step, 0], zpeer(1)),
-            remote(sd, sd, dg_ss.at[d, step, 1], dg_rs.at[d, step, 1], zpeer(nz - 1)),
-        ]
+        res = []
+        for i, (off, far, n) in enumerate(relays[step]):
+            rows = pl.ds(lax.rem(z + off + nz, nz) * CH, CH)
+            part = dg.at[d, :, rows] if n is None else dg.at[d, n, rows]
+            res.append(remote(part, part, dg_ss.at[d, step, i], dg_rs.at[d, step, i], zpeer(far + nz)))
+        return res
 
     def dg_step(lev, step):
-        if step >= half_steps or lev > 2:
+        if step >= len(relays) or lev > 2:
             return
         if step > 0:
             arrived("dg", lev, step - 1)
@@ -274,7 +323,7 @@
             c.start()
 
     def dg_finish(lev):
-        arrived("dg", lev, half_steps - 1)
+        arrived("dg", lev, len(relays) - 1)
         for n in both:
             dgt[lev - 1, core, n] = jnp.transpose(dg[lev - 1, n])
         sib_send(DGT + lev, dgt.at[lev - 1, core], dgt.at[lev - 1, core])
@@ -302,14 +351,16 @@
             lax.fori_loop(0, CH // 8, step, 0)
         sib_send(PAN + lev, pan_v.at[lev, core], pan_v.at[lev, core])
 
-    def gather(lev, level_to, p, b):
-        t = level_to * count + b * 4 + p * 2
-        e = [None, None]
-        for j in both:
+    def gather(lev, level_to, u, b):
+        t = level_to * count + b * 4
+        e = []
+        for j in range(4):
+            acc = None
             for m in range(4):
-                block = dbuf[lev, m, tbl_s[m // 2, 2 * lev + m % 2, t + j]]
-                e[j] = block if m == 0 else e[j] + block
-        return jnp.where(low, e[0], e[1])
+                block = dbuf[lev, u, m, tbl_s[m // 2, 2 * lev + m % 2, t + j]]
+                acc = block if m == 0 else acc + block
+            e.append(acc)
+        return quarters(*e)
 
     def spread(lev, level_to, p):
         group = min(chips, 4)
@@ -328,17 +379,18 @@
 
         lax.fori_loop(0, chips // group, step, 0, unroll=True)
 
-    def solve(lev, p):
-        arrived("ag", lev, p)
-        a = ag[lev, p]
+    def solve(lev, u, a):
         if lev > 0:
-            a = jnp.where(low, dot(dgt[lev - 1, p, 0], a), dot(dgt[lev - 1, p, 1], a))
+            arrived("ag", lev, u)
+            r = ag[lev, u]
+            a = quarters(*[dot(dgt[lev - 1, m // 2, m % 2], r) for m in range(4)])
             tmp[...] = a
-            yv[lev - 1, p] = tmp[mine]
-        ar = pltpu.roll(a, HALF, 1)
-        for n, an in ((0, jnp.where(low, a, ar)), (1, jnp.where(low, ar, a))):
-            d = dot(pan_v[lev, p, n].reshape(KB * CH, width), an)
-            dbuf[lev, 2 * p + n, pl.ds(0, KB)] = d.reshape(KB, CH, LANES)
+            yv[lev - 1, u] = tmp[mine]
+        turned = [turn(a, k) for k in range(4)]
+        for m in range(4):
+            am = quarters(*[turned[(j - m) % 4] for j in range(4)])
+            d = dot(pan_v[lev, m // 2, m % 2].reshape(KB * CH, width), am)
+            dbuf[lev, u, m, pl.ds(0, KB)] = d.reshape(KB, CH, LANES)
 
     def xy_send(lev, p):
         due["xy", lev, p] = lambda: wait_bytes(xy.at[lev, p], xy_rs.at[lev, p])
@@ -357,17 +409,17 @@
     pl.semaphore_wait(barrier, 2 * (nz - 1) + len(offsets) + 1)
 
     for s in both:
-        rs_send(0, s)
+        rs_send(s)
     sib_send(TBL, tbl_v.at[core], tbl_v.at[core])
-    sib_send(RHS, rp.at[1 - core, pl.ds(1, LEVELS - 1)], rq.at[core])
+    sib_send(RHS, rp.at[1 - core, pl.ds(1, LEVELS - 1)], rqp.at[core])
     sib_send(INV, dinv_v.at[LEVELS - 1], dinv_x.at[core])
-    rq[core] = rp[core, pl.ds(1, LEVELS - 1)]
+    rqp[core] = rp[core, pl.ds(1, LEVELS - 1)]
     dinv_x[core] = dinv_v[LEVELS - 1]
     dg_step(1, 0)
     combine_panels(0)
     first = []
     for s in both:
-        val = rs_finish(0, s)
+        val = rs_finish(s)
         ag_first(s, val)
         first.append(val)
     dg_step(1, 1)
@@ -375,43 +427,52 @@
     arrived("sib", TBL)
     c_tbl = pltpu.make_async_copy(tbl_v, tbl_s, loc.at[5])
     c_tbl.start()
+    due["tbl",] = c_tbl.wait
     combine_panels(1)
     combine_panels(2)
-    c_tbl.wait()
+    arrived("tbl")
     arrived("sib", RHS)
     arrived("sib", INV)
+    for lev in range(LEVELS - 1):
+        rq[0, lev], rq[1, lev] = to_streams(rqp[0, lev], rqp[1, lev])
     for lev in range(LEVELS - 1):
         arrived("sib", PAN + lev)
         if lev > 0:
             arrived("sib", DGT + lev)
-        solve(lev, 0)
+        if lev == 0:
+            arrived("ag", 0, 0)
+            arrived("ag", 0, 1)
+            start = to_streams(ag[0, 0], ag[0, 1])
+        for u in both:
+            solve(lev, u, start[u])
+            spread(lev, lev + 1, u)
+            xy_send(lev, u)
         dg_step(lev + 1, 2)
-        solve(lev, 1)
-        for p in both:
-            spread(lev, lev + 1, p)
-            xy_send(lev, p)
-        dg_step(lev + 1, 3)
         dg_step(lev + 2, 0)
         if lev > 0:
-            sib_send(ANS + lev, yv.at[lev - 1, 1 - core], yx.at[lev - 1])
+            packs = to_packs(yv[lev - 1, 0], yv[lev - 1, 1])
+            yo[lev - 1, 0] = jnp.where(core == 0, packs[0], packs[1])
+            yo[lev - 1, 1] = jnp.where(core == 0, packs[1], packs[0])
+            sib_send(ANS + lev, yo.at[lev - 1, 1], yx.at[lev - 1])
         for to in range(lev + 2, LEVELS):
             for p in both:
                 spread(lev, to, p)
         if lev < LEVELS - 2:
-            dg_finish(lev + 1)
             for p in both:
                 ag_send(lev + 1, p, residual(lev, p))
+            dg_finish(lev + 1)
             dg_step(lev + 2, 1)
         else:
             for p in both:
-                r = residual(lev, p)
-                rs_src[1, p] = jnp.where(low, dot_t(dinv_x[p, 0], r), dot_t(dinv_x[p, 1], r))
-                rs_send(1, p)
+                fs_send(p, residual(lev, p))
     for lev in (1, 2):
         arrived("sib", ANS + lev)
-        own, other = yv[lev - 1, core], yx[lev - 1]
+        own, other = yo[lev - 1, 0], yx[lev - 1]
         write(lev, jnp.where(core == 0, own, other), jnp.where(core == 0, other, own))
-    write(LEVELS - 1, rs_finish(1, 0), rs_finish(1, 1))
+    last = [fs_finish(0), fs_finish(1)]
+    write(LEVELS - 1, *[
+        quarters(last[0][h], turn(last[1][h], 1), turn(last[0][h], 1), turn(last[1][h], 2)) for h in both
+    ])
 
     for wait in sent:
         wait()
@@ -427,7 +488,6 @@
     f32 = jnp.float32
     dma = pltpu.SemaphoreType.DMA
     vmem = pltpu.VMEM
-    hops = nz // 2
     solved = LEVELS - 1
     hbm = pl.BlockSpec(memory_space=pltpu.HBM)
     return pl.pallas_call(
@@ -445,25 +505,31 @@
             pltpu.SMEM((2, 8, LEVELS * count), jnp.int32),
             vmem((2, LEVELS, CH, LANES), f32),
             vmem((2, solved, CH, LANES), f32),
-            vmem((2, 2, width, LANES), f32),
-            vmem((2, 2, nz, CH, LANES), f32),
+            vmem((2, solved, CH, LANES), f32),
+            vmem((2, width, LANES), f32),
+            vmem((2, nz, CH, LANES), f32),
+            vmem((2, 2, nz, CH // 2, LANES), f32),
+            vmem((2, 2, nz, CH // 2, LANES), f32),
             vmem((2, CH, LANES), f32),
             vmem((solved, 2, width, LANES), f32),
             vmem((2, 2, width, width), f32),
             vmem((2, 2, 2, width, width), f32),
-            vmem((solved, 4, KB + 1, CH, LANES), f32),
+            vmem((solved, 2, 4, KB + 1, CH, LANES), f32),
             vmem((solved, 2, chips, CH, LANES), f32),
             vmem((solved, 2, chips - 1, CH, LANES), f32),
             vmem((width, LANES), f32),
             vmem((2, 2, CH, LANES), f32),
+            vmem((2, 2, CH, LANES), f32),
             vmem((2, CH, LANES), f32),
             dma((7,)),
+            dma((2, nz)),
+            dma((2, nz)),
             dma((2, 2, nz)),
             dma((2, 2, nz)),
             dma((solved, 2)),
             dma((solved, 2)),
-            dma((2, hops, 2)),
-            dma((2, hops, 2)),
+            dma((2, 3, 4)),
+            dma((2, 3, 4)),
             dma((solved, 2)),
             dma((solved, 2)),
             dma((SIBS,)),

time: 70.3 us -> 67.7 us (0.963)
  Pallas kernels: 68.5 us -> 65.8 us
    pallas_call x1, Pallas kernels: 68.5 us -> 65.8 us  [shards(): pl.pallas_call(functools.partial(kernel, nx, ny, nz), out_shape=jax.Shape...]
where the time goes in v3:
time: 67.7 us; the launch traced here: 67.3 us
  Pallas kernels  65.8 us (97%)
  local copies, waits for them, and re-layouts  1.57 us (2%)
    pallas_call x1, Pallas kernels, shards(): pl.pallas_call(functools.partial(kernel, nx, ny, nz), out_shape=jax.Shape...  65.8 us
    unnamed x1, local copies, waits for them, and re-layouts  1.57 us

profile of v3, /device:TPU:1, one launch (start us, length us, event | category | flops | bytes accessed | tf_op | source)
XLA Modules:
  0.0 67.3 jit_solution(911029696959633373)
XLA Ops:
  0.0 65.8 %shard_map.46 = f32[4,2,32,128]{3,2,1,0:T(8,128)} custom-call(f32[4,2,32,128]{3,2,1,0:T(8,128)} %rhs_hbm.1, f32[4,2,32,256]{3,2,1,0:T(8,128)} %bitcast.1, f32[3,2,8,32,256]{4,3,2,1,0:T(8,128)} %pan_hbm.1, s32[3,2,8]{2,1,0:T(2,128)} %tgt_hbm.1), custom_call_target="tpu_custom_call" | custom-call | tf_op jit(solution)/shard_map/pallas_call | solution.py:493
  65.8 1.6 %copy.6 = f32[4,2,32,128]{3,2,1,0:T(8,128)} copy(f32[4,2,32,128]{3,2,1,0:T(8,128)} %shard_map.46) | data formatting | bytes 262144

commit v4 on v3

--- a/solution.py
+++ b/solution.py
@@ -20,8 +20,7 @@
     return hi, (a - hi.astype(jnp.float32)).astype(jnp.bfloat16)
 
 
-def dot3(a, b, dims):
-    ah, al = split(a)
+def dot3(ah, al, b, dims=((1,), (0,))):
     bh, bl = split(b)
     f = functools.partial(
         lax.dot_general, dimension_numbers=(dims, ((), ())), preferred_element_type=jnp.float32
@@ -31,19 +30,15 @@
     return wide[:, :n] + (wide[:, n:] + f(al, bh))
 
 
-def dot(a, b):
-    return dot3(a, b, ((1,), (0,)))
-
-
 def dot_t(a, b):
-    return dot3(a, b, ((0,), (0,)))
+    return dot3(*split(a), b, ((0,), (0,)))
 
 
 def kernel(
     nx, ny, nz,
     rhs_hbm, dinv_hbm, pan_hbm, tgt_hbm, out,
     tgt, rhs_v, dinv_v, dinv_x, pan_v, tbl_v, tbl_s, rp, rqp, rq, rs_src, rs_dst, fs_src, fs_dst, av, ag, dg, dgt,
-    dbuf, dense, xy, tmp, yv, yo, yx,
+    dbuf, dense, xy, tmp, yv, yo, yx, ps, ds,
     loc, rs_ss, rs_rs, fs_ss, fs_rs, ag_ss, ag_rs, dg_ss, dg_rs, xy_ss, xy_rs, sib_ss, sib_rs,
 ):
     chips = nx * ny
@@ -379,25 +374,46 @@
 
         lax.fori_loop(0, chips // group, step, 0, unroll=True)
 
-    def solve(lev, u, a):
+    def split_panels(lev):
+        arrived("sib", PAN + lev)
+        for m in range(4):
+            ps[lev, m, 0], ps[lev, m, 1] = split(pan_v[lev, m // 2, m % 2].reshape(KB * CH, width))
+
+    def split_inverse(lev):
+        arrived("sib", DGT + lev)
+        for m in range(4):
+            ds[m, 0], ds[m, 1] = split(dgt[lev - 1, m // 2, m % 2])
+
+    def solve(lev, u):
         if lev > 0:
-            arrived("ag", lev, u)
-            r = ag[lev, u]
-            a = quarters(*[dot(dgt[lev - 1, m // 2, m % 2], r) for m in range(4)])
+            wait_bytes(chunks(lev, u, nz - 1), ag_rs.at[lev, u])
+        r = a = ag[lev, u]
+        if lev > 0:
+            a = quarters(*[dot3(ds[m, 0], ds[m, 1], r) for m in range(4)])
             tmp[...] = a
             yv[lev - 1, u] = tmp[mine]
         turned = [turn(a, k) for k in range(4)]
         for m in range(4):
             am = quarters(*[turned[(j - m) % 4] for j in range(4)])
-            d = dot(pan_v[lev, m // 2, m % 2].reshape(KB * CH, width), am)
+            d = dot3(ps[lev, m, 0], ps[lev, m, 1], am)
             dbuf[lev, u, m, pl.ds(0, KB)] = d.reshape(KB, CH, LANES)
 
-    def xy_send(lev, p):
-        due["xy", lev, p] = lambda: wait_bytes(xy.at[lev, p], xy_rs.at[lev, p])
-        sent.append(lambda: wait_bytes(xy.at[lev, p], xy_ss.at[lev, p]))
-        for i, (dx, dy) in enumerate(offsets):
-            peer, dev = xypeer(dx, dy)
-            remote(dense.at[lev, p, peer], xy.at[lev, p, i], xy_ss.at[lev, p], xy_rs.at[lev, p], dev).start()
+    def spread_send(lev, u):
+        places = [(i, *xypeer(dx, dy)) for i, (dx, dy) in enumerate(offsets)]
+        places.append((None, chip, None))
+        for g in range(0, len(places), 4):
+            group = places[g : g + 4]
+            vals = []
+            for _, b, _ in group:
+                val = gather(lev, lev + 1, u, b)
+                vals.append(val + dense[lev, u, b] if lev > 0 else val)
+            for (_, b, _), val in zip(group, vals):
+                dense[lev, u, b] = val
+            for i, b, dev in group:
+                if i is not None:
+                    remote(
+                        dense.at[lev, u, b], xy.at[lev, u, i], xy_ss.at[lev, u], xy_rs.at[lev, u], dev
+                    ).start()
 
     def residual(lev, p):
         arrived("xy", lev, p)
@@ -431,22 +447,27 @@
     combine_panels(1)
     combine_panels(2)
     arrived("tbl")
+    split_panels(0)
     arrived("sib", RHS)
     arrived("sib", INV)
     for lev in range(LEVELS - 1):
         rq[0, lev], rq[1, lev] = to_streams(rqp[0, lev], rqp[1, lev])
     for lev in range(LEVELS - 1):
-        arrived("sib", PAN + lev)
-        if lev > 0:
-            arrived("sib", DGT + lev)
         if lev == 0:
             arrived("ag", 0, 0)
             arrived("ag", 0, 1)
-            start = to_streams(ag[0, 0], ag[0, 1])
+            ag[0, 0], ag[0, 1] = to_streams(ag[0, 0], ag[0, 1])
+
+        def work(u, _, lev=lev):
+            solve(lev, u)
+            spread_send(lev, u)
+            return 0
+
+        lax.fori_loop(0, 2, work, 0)
         for u in both:
-            solve(lev, u, start[u])
-            spread(lev, lev + 1, u)
-            xy_send(lev, u)
+            due.pop(("ag", lev, u), None)
+            due["xy", lev, u] = lambda lev=lev, u=u: wait_bytes(xy.at[lev, u], xy_rs.at[lev, u])
+            sent.append(lambda lev=lev, u=u: wait_bytes(xy.at[lev, u], xy_ss.at[lev, u]))
         dg_step(lev + 1, 2)
         dg_step(lev + 2, 0)
         if lev > 0:
@@ -455,13 +476,18 @@
             yo[lev - 1, 1] = jnp.where(core == 0, packs[1], packs[0])
             sib_send(ANS + lev, yo.at[lev - 1, 1], yx.at[lev - 1])
         for to in range(lev + 2, LEVELS):
-            for p in both:
-                spread(lev, to, p)
+            def later(u, _, lev=lev, to=to):
+                spread(lev, to, u)
+                return 0
+
+            lax.fori_loop(0, 2, later, 0)
         if lev < LEVELS - 2:
+            split_panels(lev + 1)
             for p in both:
                 ag_send(lev + 1, p, residual(lev, p))
             dg_finish(lev + 1)
             dg_step(lev + 2, 1)
+            split_inverse(lev + 1)
         else:
             for p in both:
                 fs_send(p, residual(lev, p))
@@ -521,6 +547,8 @@
             vmem((2, 2, CH, LANES), f32),
             vmem((2, 2, CH, LANES), f32),
             vmem((2, CH, LANES), f32),
+            vmem((solved, 4, 2, KB * CH, width), jnp.bfloat16),
+            vmem((4, 2, width, width), jnp.bfloat16),
             dma((7,)),
             dma((2, nz)),
             dma((2, nz)),

time: 67.7 us -> 69.8 us (1.031)
  Pallas kernels: 65.8 us -> 68.1 us
    pallas_call x1, Pallas kernels: 65.8 us -> 68.1 us  [shards(): pl.pallas_call(functools.partial(kernel, nx, ny, nz), out_shape=jax.Shape...]
where the time goes in v4:
time: 69.8 us; the launch traced here: 69.7 us
  Pallas kernels  68.1 us (98%)
  local copies, waits for them, and re-layouts  1.57 us (2%)
    pallas_call x1, Pallas kernels, shards(): pl.pallas_call(functools.partial(kernel, nx, ny, nz), out_shape=jax.Shape...  68.1 us
    unnamed x1, local copies, waits for them, and re-layouts  1.57 us

profile of v4, /device:TPU:1, one launch (start us, length us, event | category | flops | bytes accessed | tf_op | source)
XLA Modules:
  0.0 69.7 jit_solution(5105359503399449310)
XLA Ops:
  0.0 68.1 %shard_map.46 = f32[4,2,32,128]{3,2,1,0:T(8,128)} custom-call(f32[4,2,32,128]{3,2,1,0:T(8,128)} %rhs_hbm.1, f32[4,2,32,256]{3,2,1,0:T(8,128)} %bitcast.1, f32[3,2,8,32,256]{4,3,2,1,0:T(8,128)} %pan_hbm.1, s32[3,2,8]{2,1,0:T(2,128)} %tgt_hbm.1), custom_call_target="tpu_custom_call" | custom-call | tf_op jit(solution)/shard_map/pallas_call | solution.py:519
  68.1 1.6 %copy.6 = f32[4,2,32,128]{3,2,1,0:T(8,128)} copy(f32[4,2,32,128]{3,2,1,0:T(8,128)} %shard_map.46) | data formatting | bytes 262144

commit v5 on v3

--- a/solution.py
+++ b/solution.py
@@ -469,13 +469,12 @@
         arrived("sib", ANS + lev)
         own, other = yo[lev - 1, 0], yx[lev - 1]
         write(lev, jnp.where(core == 0, own, other), jnp.where(core == 0, other, own))
+    for wait in sent:
+        wait()
     last = [fs_finish(0), fs_finish(1)]
     write(LEVELS - 1, *[
         quarters(last[0][h], turn(last[1][h], 1), turn(last[0][h], 1), turn(last[1][h], 2)) for h in both
     ])
-
-    for wait in sent:
-        wait()
 
 
 TBL, RHS, INV, AV, PAN, DGT, ANS, SIBS = 0, 1, 2, 3, 4, 6, 8, 11

time: 67.7 us -> 67.6 us (level)
  no operation moved by 1% of the time
where the time goes in v5:
time: 67.6 us; the launch traced here: 67.2 us
  Pallas kernels  65.6 us (97%)
  local copies, waits for them, and re-layouts  1.57 us (2%)
    pallas_call x1, Pallas kernels, shards(): pl.pallas_call(functools.partial(kernel, nx, ny, nz), out_shape=jax.Shape...  65.6 us
    unnamed x1, local copies, waits for them, and re-layouts  1.57 us

profile of v5, /device:TPU:1, one launch (start us, length us, event | category | flops | bytes accessed | tf_op | source)
XLA Modules:
  0.0 67.2 jit_solution(823375254231326383)
XLA Ops:
  0.0 65.6 %shard_map.46 = f32[4,2,32,128]{3,2,1,0:T(8,128)} custom-call(f32[4,2,32,128]{3,2,1,0:T(8,128)} %rhs_hbm.1, f32[4,2,32,256]{3,2,1,0:T(8,128)} %bitcast.1, f32[3,2,8,32,256]{4,3,2,1,0:T(8,128)} %pan_hbm.1, s32[3,2,8]{2,1,0:T(2,128)} %tgt_hbm.1), custom_call_target="tpu_custom_call" | custom-call | tf_op jit(solution)/shard_map/pallas_call | solution.py:492
  65.6 1.6 %copy.6 = f32[4,2,32,128]{3,2,1,0:T(8,128)} copy(f32[4,2,32,128]{3,2,1,0:T(8,128)} %shard_map.46) | data formatting | bytes 262144

commit v6 on v5

--- a/solution.py
+++ b/solution.py
@@ -454,14 +454,17 @@
             yo[lev - 1, 0] = jnp.where(core == 0, packs[0], packs[1])
             yo[lev - 1, 1] = jnp.where(core == 0, packs[1], packs[0])
             sib_send(ANS + lev, yo.at[lev - 1, 1], yx.at[lev - 1])
-        for to in range(lev + 2, LEVELS):
+        if lev + 2 < LEVELS:
             for p in both:
-                spread(lev, to, p)
+                spread(lev, lev + 2, p)
         if lev < LEVELS - 2:
             for p in both:
                 ag_send(lev + 1, p, residual(lev, p))
             dg_finish(lev + 1)
             dg_step(lev + 2, 1)
+            for to in range(lev + 3, LEVELS):
+                for p in both:
+                    spread(lev, to, p)
         else:
             for p in both:
                 fs_send(p, residual(lev, p))

time: 67.6 us -> 67.6 us (level)
  no operation moved by 1% of the time
where the time goes in v6:
time: 67.6 us; the launch traced here: 67.2 us
  Pallas kernels  65.6 us (97%)
  local copies, waits for them, and re-layouts  1.57 us (2%)
    pallas_call x1, Pallas kernels, shards(): pl.pallas_call(functools.partial(kernel, nx, ny, nz), out_shape=jax.Shape...  65.6 us
    unnamed x1, local copies, waits for them, and re-layouts  1.57 us

profile of v6, /device:TPU:1, one launch (start us, length us, event | category | flops | bytes accessed | tf_op | source)
XLA Modules:
  0.0 67.2 jit_solution(16096121332518703638)
XLA Ops:
  0.0 65.6 %shard_map.46 = f32[4,2,32,128]{3,2,1,0:T(8,128)} custom-call(f32[4,2,32,128]{3,2,1,0:T(8,128)} %rhs_hbm.1, f32[4,2,32,256]{3,2,1,0:T(8,128)} %bitcast.1, f32[3,2,8,32,256]{4,3,2,1,0:T(8,128)} %pan_hbm.1, s32[3,2,8]{2,1,0:T(2,128)} %tgt_hbm.1), custom_call_target="tpu_custom_call" | custom-call | tf_op jit(solution)/shard_map/pallas_call | solution.py:495
  65.6 1.6 %copy.6 = f32[4,2,32,128]{3,2,1,0:T(8,128)} copy(f32[4,2,32,128]{3,2,1,0:T(8,128)} %shard_map.46) | data formatting | bytes 262144
